TPU v7x, 32 devices: a whole 2x2x4 slice. The times are simulated.
32 devices in a mesh: req: 4 (over z), seq: 8 (over y, x, core).
Axes of the slice: x: 2, y: 2, z: 4, core: 2. Of those that a mesh axis runs over, the one named last changes fastest.
Arguments:
- hidden_in: bfloat16 [8, 256, 2048], P('req', 'seq'), may hold values from -6 to 6
- norm_gain: float32 [2048], replicated, may hold values from 0.1 to 1.9
- w_query: bfloat16 [2048, 1024], P(('req', 'seq')), may hold values from -0.125 to 0.125
- w_key: bfloat16 [2048, 512], P(('req', 'seq')), may hold values from -0.3125 to 0.3125
- w_value: bfloat16 [2048, 512], P(('req', 'seq')), may hold values from -0.125 to 0.125
- cache_keys: bfloat16 [8, 2048, 512], P('req', 'seq'), may hold values from -525 to 525
- cache_values: bfloat16 [8, 2048, 512], P('req', 'seq'), may hold values from -6 to 6
- cache_lengths: int32 [8], P('req'), may hold values from 1 to 2048, as said below
Outputs:
- attended: bfloat16 [8, 256, 1024], P('req', 'seq')
- new_keys: bfloat16 [8, 256, 512], P('req', 'seq')
- new_values: bfloat16 [8, 256, 512], P('req', 'seq')
Inputs may be any that keep to these rules, and one draw needn't show every extreme that they name: `cache_lengths`: some request's cache holds exactly 2048 positions.
All inputs are finite; a program needn't handle non-finite values.
Results may differ from a plain program's by a relative error of at most 0.034.
Values may be sent and summed in bfloat16 or wider, within the bound.
A program may use at most 128 MiB of HBM per device.

v0:
```python
import jax
import jax.numpy as jnp
from jax import lax
from jax.sharding import PartitionSpec as P

HEADS = 4
KV_HEADS = 2
HEAD = 256


EPSILON = 1e-06
THETA = 1000042.0
MASKED = -1e30


def tables(positions, head_size):
    half_size = head_size // 2
    frequency = THETA ** (-(jnp.arange(half_size, dtype=jnp.float32) * 2.0 / head_size))
    angles = positions.astype(jnp.float32)[..., None] * frequency
    return (jnp.cos(angles)[..., None, :], jnp.sin(angles)[..., None, :])


def rotate(values, cosine, sine_part):
    half_size = values.shape[-1] // 2
    first_half = values[..., :half_size]
    second_half = values[..., half_size:]
    return jnp.concatenate(
        [
            first_half * cosine - second_half * sine_part,
            second_half * cosine + first_half * sine_part,
        ],
        axis=-1,
    )


def attend(query_rows, key_rows, value_rows, live):
    span_len = query_rows.shape[0]
    group_size = HEADS // KV_HEADS
    query_view = query_rows.reshape(span_len, KV_HEADS, group_size, HEAD)
    key_view = key_rows.reshape(key_rows.shape[0], KV_HEADS, HEAD)
    value_view = value_rows.reshape(value_rows.shape[0], KV_HEADS, HEAD)
    scores = jnp.einsum(
        "cgeh,kgh->cgek", query_view, key_view, preferred_element_type=jnp.float32
    ) * HEAD ** (-0.5)
    mask_view = live[:, None, None, :]
    scores = jnp.where(mask_view, scores, MASKED)
    block_max = jnp.max(scores, axis=-1)
    weights = jnp.where(mask_view, jnp.exp(scores - block_max[..., None]), 0.0)
    block_sum = jnp.sum(weights, axis=-1)
    block_out = jnp.einsum(
        "cgek,kgh->cgeh",
        weights.astype(jnp.bfloat16),
        value_view,
        preferred_element_type=jnp.float32,
    )
    return (
        block_max.reshape(span_len, HEADS),
        block_sum.reshape(span_len, HEADS),
        block_out.reshape(span_len, HEADS * HEAD).astype(jnp.bfloat16),
    )


def attend_rows(query_rows, key_rows, value_rows, live):
    total_rows = query_rows.shape[0]
    row_block = min(512, total_rows)
    pieces = []
    for begin in range(0, total_rows, row_block):
        pieces.append(
            attend(
                query_rows[begin : begin + row_block],
                key_rows,
                value_rows,
                live[begin : begin + row_block],
            )
        )
    return tuple((jnp.concatenate([piece[slot] for piece in pieces], axis=0) for slot in range(3)))


def body(hidden_in, norm_gain, w_query, w_key, w_value, cache_keys, cache_values, cache_lengths):
    seq_count = lax.axis_size("seq")
    seq_seat = lax.axis_index("seq")
    req_local, slice_len, model_width = hidden_in.shape
    cache_len_dev = cache_keys.shape[1]
    span_len = slice_len * seq_count
    inputs = hidden_in.astype(jnp.float32)
    normed = (
        inputs * lax.rsqrt(jnp.mean(inputs * inputs, axis=-1, keepdims=True) + EPSILON) * norm_gain
    ).astype(jnp.bfloat16)
    flat_rows = normed.reshape(req_local * slice_len, model_width)
    full_query, full_key, full_value = (
        lax.all_gather(w_query, ("req", "seq"), axis=0, tiled=True),
        lax.all_gather(w_key, ("req", "seq"), axis=0, tiled=True),
        lax.all_gather(w_value, ("req", "seq"), axis=0, tiled=True),
    )
    query_raw = jnp.dot(flat_rows, full_query, preferred_element_type=jnp.float32)
    key_raw = jnp.dot(flat_rows, full_key, preferred_element_type=jnp.float32)
    value_raw = jnp.dot(flat_rows, full_value, preferred_element_type=jnp.float32)
    local_index = jnp.arange(slice_len, dtype=jnp.int32)
    positions = cache_lengths[:, None] + seq_seat * slice_len + local_index[None, :]
    cosine, sine_part = tables(positions, HEAD)
    queries = (
        rotate(query_raw.reshape(req_local, slice_len, HEADS, HEAD), cosine, sine_part)
        .reshape(req_local, slice_len, HEADS * HEAD)
        .astype(jnp.bfloat16)
    )
    new_keys = (
        rotate(key_raw.reshape(req_local, slice_len, KV_HEADS, HEAD), cosine, sine_part)
        .reshape(req_local, slice_len, KV_HEADS * HEAD)
        .astype(jnp.bfloat16)
    )
    new_values = value_raw.reshape(req_local, slice_len, KV_HEADS * HEAD).astype(jnp.bfloat16)
    all_queries = lax.all_gather(queries, "seq", axis=1, tiled=True)
    key_block = jnp.concatenate([cache_keys, new_keys], axis=1)
    value_block = jnp.concatenate([cache_values, new_values], axis=1)
    span_index = jnp.arange(span_len, dtype=jnp.int32)
    cache_pos = seq_seat * cache_len_dev + jnp.arange(cache_len_dev, dtype=jnp.int32)
    new_pos = seq_seat * slice_len + local_index
    new_live = new_pos[None, :] <= span_index[:, None]
    max_list = []
    sum_list = []
    out_list = []
    for request in range(req_local):
        cache_live = cache_pos < cache_lengths[request]
        live_full = jnp.concatenate(
            [jnp.broadcast_to(cache_live[None, :], (span_len, cache_len_dev)), new_live], axis=1
        )
        query_rows = all_queries[request]
        terms = attend_rows(query_rows, key_block[request], value_block[request], live_full)
        max_list.append(terms[0])
        sum_list.append(terms[1])
        out_list.append(terms[2])
    max_all = jnp.stack(max_list)
    sum_all = jnp.stack(sum_list)
    out_all = jnp.stack(out_list)
    got_max, got_sum = (
        lax.all_to_all(max_all, "seq", split_axis=1, concat_axis=0, tiled=True),
        lax.all_to_all(sum_all, "seq", split_axis=1, concat_axis=0, tiled=True),
    )
    got_out = lax.all_to_all(out_all, "seq", split_axis=1, concat_axis=0, tiled=True)
    got_max = got_max.reshape(seq_count, req_local, slice_len, HEADS)
    got_sum = got_sum.reshape(seq_count, req_local, slice_len, HEADS)
    got_out = got_out.reshape(seq_count, req_local, slice_len, HEADS, HEAD)
    best_max = jnp.max(got_max, axis=0)
    factor = jnp.exp(got_max - best_max)
    total_sum = jnp.sum(got_sum * factor, axis=0)
    total_out = jnp.sum(got_out.astype(jnp.float32) * factor[..., None], axis=0)
    attended = (
        (total_out / total_sum[..., None])
        .reshape(req_local, slice_len, HEADS * HEAD)
        .astype(jnp.bfloat16)
    )
    return (attended, new_keys, new_values)


def solution(mesh):
    in_specs = (
        P("req", "seq", None),
        P(),
        P(("req", "seq"), None),
        P(("req", "seq"), None),
        P(("req", "seq"), None),
        P("req", "seq", None),
        P("req", "seq", None),
        P("req"),
    )
    out_specs = (P("req", "seq", None), P("req", "seq", None), P("req", "seq", None))
    return jax.shard_map(body, mesh=mesh, in_specs=in_specs, out_specs=out_specs, check_vma=False)
```

profile of v0, /device:TPU:0, one launch (start us, length us, event | category | flops | bytes accessed | tf_op | source)
XLA Modules:
  0.0 268.6 jit_solution(17142669975627491575)
XLA Ops:
  9.5 1.3 fusion.51
  10.8 1.3 fusion.41
  12.1 1.1 constant_dynamic-update-slice_fusion.1
  13.6 62.0 %all-gather.9.cloned.1.call-done = bf16[2048,1024]{1,0:T(8,128)(2,1)} async-done(((bf16[64,1024]{1,0:T(8,128)(2,1)}), bf16[2048,1024]{1,0:T(8,128)(2,1)}) %all-gather.9.cloned.1.call-update) | async-done | bytes 4194320 | tf_op jit(solution)/shard_map/all_gather | solution.py:91
  75.6 6.5 %copy.67 = bf16[1024,2048]{1,0:T(8,128)(2,1)} copy(bf16[1024,2048]{0,1:T(8,128)(2,1)} %bitcast.92) | data formatting | bytes 8388608 | tf_op jit(solution)/shard_map/dot_general | solution.py:95
  82.2 3.6 %fusion.31 = f32[2,32,4,256]{3,1,2,0:T(8,128)S(1)} fusion(bf16[4,256,2048,1]{2,1,0,3:T(8,128)(2,1)} %bitcast.90, bf16[2,32,2048]{2,1,0:T(8,128)(2,1)S(1)} %copy-done, f32[2048]{0:T(1024)S(1)} %copy-done.6, f32[2,32]{1,0:T(2,128)S(1)} %add_rsqrt_fusion), kind=kOutput, calls=%fused_computation.42 | convolution fusion | flops 268959744 | bytes 4727040 | tf_op jit(solution)/shard_map/dot_general | solution.py:95
  86.8 46.7 %all-gather.7.cloned.1.call-done = bf16[2048,512]{1,0:T(8,128)(2,1)} async-done(((bf16[64,512]{1,0:T(8,128)(2,1)}), bf16[2048,512]{1,0:T(8,128)(2,1)}) %all-gather.7.cloned.1.call-update) | async-done | bytes 2097168 | tf_op jit(solution)/shard_map/all_gather | solution.py:92
  133.5 2.9 %copy.65 = bf16[512,2048]{1,0:T(8,128)(2,1)S(1)} copy(bf16[512,2048]{0,1:T(8,128)(2,1)} %bitcast.94) | data formatting | bytes 4194304 | tf_op jit(solution)/shard_map/dot_general | solution.py:96
  138.8 52.8 %all-gather.5.cloned.1.call-done = bf16[2048,512]{1,0:T(8,128)(2,1)} async-done(((bf16[64,512]{1,0:T(8,128)(2,1)}), bf16[2048,512]{1,0:T(8,128)(2,1)}) %all-gather.5.cloned.1.call-update) | async-done | bytes 2097168 | tf_op jit(solution)/shard_map/all_gather | solution.py:93
  191.6 2.1 fusion.8
  193.8 0.8 reshape_squeeze.21
  194.6 0.8 reshape_squeeze.18
  195.4 20.9 %all-gather.11.cloned.1.call-done = bf16[2,256,1024]{2,1,0:T(8,128)(2,1)} async-done(((bf16[2,32,1024]{2,1,0:T(8,128)(2,1)}), bf16[2,256,1024]{2,1,0:T(8,128)(2,1)}) %all-gather.11.cloned.1.call-update) | async-done | bytes 1048592 | tf_op jit(solution)/shard_map/all_gather | solution.py:112
  216.3 1.3 fusion.49
  219.8 1.3 fusion.53
  222.0 1.0 reshape.133
  223.0 4.1 %all-to-all-start.2 = ((f32[8,1,256]{2,1,0:T(1,128)}), f32[8,1,256]{2,1,0:T(1,128)}, u32[]{:S(2)}, u32[]{:S(2)}) async-start(f32[8,1,256]{2,1,0:T(1,128)} %reshape.133), calls=%async_computation.2 | async-start | bytes 16384 | tf_op jit(solution)/shard_map/all_to_all | solution.py:137
  227.0 1.5 convolution_convert_fusion
  228.5 1.3 convolution_convert_fusion.1
  230.1 0.9 reshape.131
  231.0 1.0 copy.78
  232.0 1.0 copy.77
  233.0 4.1 %all-to-all-start.1 = ((f32[8,1,256]{2,1,0:T(1,128)}), f32[8,1,256]{2,1,0:T(1,128)S(1)}, u32[]{:S(2)}, u32[]{:S(2)}) async-start(f32[8,1,256]{2,1,0:T(1,128)} %reshape.131), calls=%async_computation.1 | async-start | bytes 16384 | tf_op jit(solution)/shard_map/all_to_all | solution.py:136
  237.1 3.2 %pad_maximum_fusion = bf16[2,256,1024]{2,0,1:T(2,128)(2,1)} fusion(bf16[1,256,1024]{2,0,1:T(2,128)(2,1)S(1)} %copy.78, bf16[1,256,1024]{2,0,1:T(2,128)(2,1)S(1)} %copy.77), kind=kLoop, calls=%fused_computation.16 | loop fusion | flops 2097152 | bytes 2097152 | tf_op jit(solution)/shard_map/stack | solution.py:134
  240.4 1.5 all-to-all-done.1
  241.9 3.7 %all-to-all-start = ((bf16[2,256,1024]{2,0,1:T(2,128)(2,1)}), bf16[2,256,1024]{2,0,1:T(2,128)(2,1)S(1)}, u32[]{:S(2)}, u32[]{:S(2)}) async-start(bf16[2,256,1024]{2,0,1:T(2,128)(2,1)} %pad_maximum_fusion), calls=%async_computation | async-start | bytes 2097152 | tf_op jit(solution)/shard_map/all_to_all | solution.py:139
  246.1 1.4 reduce.1
  249.8 1.9 mul.157
  251.7 2.3 mul.158
  254.1 0.8 div.27
  255.0 1.1 div.28
  256.1 4.7 %all-to-all-done = bf16[2,256,1024]{2,0,1:T(2,128)(2,1)S(1)} async-done(((bf16[2,256,1024]{2,0,1:T(2,128)(2,1)}), bf16[2,256,1024]{2,0,1:T(2,128)(2,1)S(1)}, u32[]{:S(2)}, u32[]{:S(2)}) %all-to-all-start) | async-done | bytes 1048608 | tf_op jit(solution)/shard_map/all_to_all | solution.py:139
  (81 shorter events, 13.5 us)
Async XLA Ops:
  7.2 6.2 %copy-start.11 = (s32[2]{0:T(128)S(1)}, s32[2]{0:T(128)}, u32[]{:S(2)}) copy-start(s32[2]{0:T(128)} %param.15) | copy-start | bytes 28
  7.2 6.0 %copy-start = (bf16[2,32,2048]{2,1,0:T(8,128)(2,1)S(1)}, bf16[2,32,2048]{2,1,0:T(8,128)(2,1)}, u32[]{:S(2)}) copy-start(bf16[2,32,2048]{2,1,0:T(8,128)(2,1)} %param.8) | copy-start | bytes 786436
  7.2 68.5 %all-gather.9.cloned.1.call-start = ((), (), s32[]{:S(2)}) async-start(), calls=%async_computation.5 | async-start | bytes 4325376 | tf_op jit(solution)/shard_map/all_gather | solution.py:91
  7.9 125.5 %all-gather.7.cloned.1.call-start = ((), (), s32[]{:S(2)}) async-start(), calls=%async_computation.4 | async-start | bytes 2162688 | tf_op jit(solution)/shard_map/all_gather | solution.py:92
  8.7 182.9 %all-gather.5.cloned.1.call-start = ((), (), s32[]{:S(2)}) async-start(), calls=%async_computation.3 | async-start | bytes 2162688 | tf_op jit(solution)/shard_map/all_gather | solution.py:93
  9.4 206.9 %all-gather.11.cloned.1.call-start = ((), (), s32[]{:S(2)}) async-start(), calls=%async_computation.6 | async-start | bytes 1179648 | tf_op jit(solution)/shard_map/all_gather | solution.py:112
  75.6 6.5 %copy-start.6 = (f32[2048]{0:T(1024)S(1)}, f32[2048]{0:T(1024)}, u32[]{:S(2)}) copy-start(f32[2048]{0:T(1024)} %param.9) | copy-start | bytes 24580
  137.2 0.6 copy-start.5
  138.8 54.9 %copy-start.2 = (bf16[2,256,512]{2,1,0:T(8,128)(2,1)S(1)}, bf16[2,256,512]{2,1,0:T(8,128)(2,1)}, u32[]{:S(2)}) copy-start(bf16[2,256,512]{2,1,0:T(8,128)(2,1)} %param.14) | copy-start | bytes 1572868
  193.7 1.6 copy-start.4
  218.1 1.7 copy-start.7
  221.1 0.7 copy-start.10
  221.1 5.9 %copy-start.8 = (f32[256,2,2]{0,2,1:T(2,128)S(1)}, f32[256,2,2]{0,2,1:T(2,128)}, u32[]{:S(2)}) copy-start(f32[256,2,2]{0,2,1:T(2,128)} %copy-done.7) | copy-start | bytes 12292
  222.9 5.6 %copy-start.3 = (bf16[288,2,256]{2,1,0:T(2,128)(2,1)S(1)}, bf16[288,2,256]{2,1,0:T(2,128)(2,1)}, u32[]{:S(2)}) copy-start(bf16[288,2,256]{2,1,0:T(2,128)(2,1)} %reshape_squeeze.18) | copy-start | bytes 884740
  223.0 10.1 %all-to-all-start.2 = ((f32[8,1,256]{2,1,0:T(1,128)}), f32[8,1,256]{2,1,0:T(1,128)}, u32[]{:S(2)}, u32[]{:S(2)}) async-start(f32[8,1,256]{2,1,0:T(1,128)} %reshape.133), calls=%async_computation.2 | async-start | bytes 16384 | tf_op jit(solution)/shard_map/all_to_all | solution.py:137
  228.5 1.3 copy-start.9
  229.9 2.1 copy-start.1
  233.0 8.8 %all-to-all-start.1 = ((f32[8,1,256]{2,1,0:T(1,128)}), f32[8,1,256]{2,1,0:T(1,128)S(1)}, u32[]{:S(2)}, u32[]{:S(2)}) async-start(f32[8,1,256]{2,1,0:T(1,128)} %reshape.131), calls=%async_computation.1 | async-start | bytes 16384 | tf_op jit(solution)/shard_map/all_to_all | solution.py:136
  241.9 18.9 %all-to-all-start = ((bf16[2,256,1024]{2,0,1:T(2,128)(2,1)}), bf16[2,256,1024]{2,0,1:T(2,128)(2,1)S(1)}, u32[]{:S(2)}, u32[]{:S(2)}) async-start(bf16[2,256,1024]{2,0,1:T(2,128)(2,1)} %pad_maximum_fusion), calls=%async_computation | async-start | bytes 2097152 | tf_op jit(solution)/shard_map/all_to_all | solution.py:139
Sparse Core Ops, SparseCore 0:
  10.9 64.7 all-gather.8
  78.5 54.9 all-gather.6
  136.3 55.2 all-gather.4
  193.9 22.3 all-gather.10
where the time goes:
time: 269 us
  waiting for transfers between devices  191 us (71%)
  local copies, waits for them, and re-layouts  31.7 us (12%)
  between operations  14.2 us (5%)
  starting transfers between devices  12.1 us (4%)
  matrix products  10.9 us (4%)
  other arithmetic  9.13 us (3%)
    all_gather x1, waiting for transfers between devices, body(): lax.all_gather(w_query, ('req', 'seq'), axis=0, tiled=True)  62 us
    all_gather x1, waiting for transfers between devices, body(): lax.all_gather(w_value, ('req', 'seq'), axis=0, tiled=True)  52.8 us
    all_gather x1, waiting for transfers between devices, body(): lax.all_gather(w_key, ('req', 'seq'), axis=0, tiled=True)  46.7 us
    all_gather x1, waiting for transfers between devices, body(): all_queries = lax.all_gather(queries, 'seq', axis=1, tiled=True)  20.9 us
    dot_general x1, local copies, waits for them, and re-layouts, body(): jnp.dot(flat_rows, full_query, preferred_element_type=jnp.float32)  6.54 us
  transfers between devices with their start and end apart: 7, of which 6 were waited for; matrix products, arithmetic and copies ran while one was open for 16% of the time, Pallas kernels for 0%

commit v1 on v0

--- a/solution.py
+++ b/solution.py
@@ -1,6 +1,11 @@
+import functools
+
 import jax
 import jax.numpy as jnp
+import numpy as np
 from jax import lax
+from jax.experimental import pallas as pl
+from jax.experimental.pallas import tpu as pltpu
 from jax.sharding import PartitionSpec as P
 
 HEADS = 4
@@ -151,6 +156,421 @@
     )
     return (attended, new_keys, new_values)
 
+MESH_ID = pl.DeviceIdType.MESH
+
+
+def fused_kernel(
+    planes,
+    x_hbm,
+    gain_ref,
+    freq_ref,
+    wq,
+    wk,
+    wv,
+    ck,
+    cv,
+    lens,
+    att,
+    nk,
+    nv,
+    xin,
+    xbuf,
+    wbuf,
+    kvbuf,
+    stage,
+    nbuf,
+    ostage,
+    sbuf,
+    cos_t,
+    sin_t,
+    xin_sem,
+    w_send,
+    w_recv,
+    z_send,
+    z_recv,
+    x_send,
+    x_recv,
+    c_send,
+    c_recv,
+    f_send,
+    f_recv,
+    n_send,
+    n_recv,
+    o_send,
+    o_recv,
+    a_send,
+    a_recv,
+):
+    me = lax.axis_index("seq")
+    plane = lax.axis_index("req")
+    chip, core = lax.div(me, 2), lax.rem(me, 2)
+    group, lane = lax.div(chip, 2), lax.rem(chip, 2)
+    sibling = chip * 2 + (1 - core)
+    slice_len = xin.shape[1]
+    span = slice_len * 8
+    w_rows = wq.shape[0]
+    block = ck.shape[1]
+    depth = w_rows * 8
+
+    def cols(index):
+        return pl.ds(pl.multiple_of(index * HEAD, HEAD), HEAD)
+
+    def remote(src, dst, ssem, rsem, peer):
+        return pltpu.make_async_remote_copy(
+            src_ref=src,
+            dst_ref=dst,
+            send_sem=ssem,
+            recv_sem=rsem,
+            device_id={"seq": peer},
+            device_id_type=MESH_ID,
+        )
+
+    def push(src, dst, ssem, rsem, peer):
+        @pl.when(peer != me)
+        def _():
+            remote(src, dst, ssem, rsem, peer).start()
+
+        @pl.when(peer == me)
+        def _():
+            pltpu.make_async_copy(src, dst, rsem).start()
+
+    def drain(src, dst, ssem, rsem, peer):
+        @pl.when(peer != me)
+        def _():
+            remote(src, dst, ssem, rsem, peer).wait_send()
+
+    def arrived(dst, rsem):
+        pltpu.make_async_copy(dst, dst, rsem).wait()
+
+    load_x = pltpu.make_async_copy(x_hbm, xin, xin_sem)
+    load_x.start()
+    barrier = pltpu.get_barrier_semaphore()
+    for d in range(1, 8):
+        pl.semaphore_signal(
+            barrier, inc=1, device_id={"seq": lax.rem(me + d, 8)}, device_id_type=MESH_ID
+        )
+    for d in range(1, planes):
+        pl.semaphore_signal(
+            barrier, inc=1, device_id={"req": lax.rem(plane + d, planes)}, device_id_type=MESH_ID
+        )
+    load_x.wait()
+    rows = xin[...].astype(jnp.float32)
+    mean = jnp.mean(rows * rows, axis=-1, keepdims=True)
+    normed = (rows * lax.rsqrt(mean + EPSILON) * gain_ref[...][None]).astype(jnp.bfloat16)
+    xbuf[:, pl.ds(pl.multiple_of(me * slice_len, slice_len), slice_len), :] = normed
+    pl.semaphore_wait(barrier, 7 + planes - 1)
+
+    def w_slot(source):
+        return wbuf.at[plane, pl.ds(pl.multiple_of(source * w_rows, w_rows), w_rows), :]
+
+    for d in list(range(1, 8)) + [0]:
+        peer = lax.rem(me + d, 8)
+        p_chip, p_core = lax.div(peer, 2), lax.rem(peer, 2)
+        p_group, p_lane = lax.div(p_chip, 2), lax.rem(p_chip, 2)
+
+        @pl.when(p_core == 0)
+        def _():
+            push(wq.at[:, cols(p_chip)], w_slot(me), w_send.at[d], w_recv.at[me], peer)
+
+        @pl.when(p_core == 1)
+        def _():
+            @pl.when(p_lane == 0)
+            def _():
+                push(wk.at[:, cols(p_group)], w_slot(me), w_send.at[d], w_recv.at[me], peer)
+
+            @pl.when(p_lane == 1)
+            def _():
+                push(wv.at[:, cols(p_group)], w_slot(me), w_send.at[d], w_recv.at[me], peer)
+
+    def x_slot(source):
+        return xbuf.at[:, pl.ds(pl.multiple_of(source * slice_len, slice_len), slice_len), :]
+
+    def x_copy(d):
+        peer = lax.rem(chip + d, 4) * 2 + core if d else sibling
+        return remote(x_slot(me), x_slot(me), x_send.at[d], x_recv.at[me], peer)
+
+    def x_forward(d):
+        source = lax.rem(chip + 4 - d, 4) * 2 + core
+        return source, remote(
+            x_slot(source), x_slot(source), x_send.at[3 + d], x_recv.at[source], sibling
+        )
+
+    for d in (1, 2, 3, 0):
+        x_copy(d).start()
+
+    def c_slot(which, source):
+        return kvbuf.at[which, pl.ds(pl.multiple_of(source * block, block), block), :]
+
+    for d in list(range(1, 8)) + [0]:
+        peer = lax.rem(me + d, 8)
+        p_chip, p_core = lax.div(peer, 2), lax.rem(peer, 2)
+        p_group, p_lane = lax.div(p_chip, 2), lax.rem(p_chip, 2)
+
+        @pl.when(p_core == 0)
+        def _():
+            push(ck.at[p_lane, :, cols(p_group)], c_slot(0, me), c_send.at[d], c_recv.at[me], peer)
+
+        @pl.when(p_core == 1)
+        def _():
+            push(cv.at[p_lane, :, cols(p_group)], c_slot(1, me), c_send.at[d], c_recv.at[me], peer)
+
+    for s in range(8):
+        arrived(w_slot(s), w_recv.at[s])
+
+    def z_copy(d):
+        return pltpu.make_async_remote_copy(
+            src_ref=wbuf.at[plane],
+            dst_ref=wbuf.at[plane],
+            send_sem=z_send.at[d],
+            recv_sem=z_recv.at[plane],
+            device_id={"req": lax.rem(plane + d, planes)},
+            device_id_type=MESH_ID,
+        )
+
+    for d in range(1, planes):
+        z_copy(d).start()
+
+    is_value = core * lane
+    turn = (1 - is_value).astype(jnp.float32)
+    for r in range(2):
+        position = lens[r] + lax.broadcasted_iota(jnp.int32, (span, HEAD // 2), 0)
+        angle = position.astype(jnp.float32) * freq_ref[...] * turn
+        cos_t[r] = jnp.cos(angle)
+        sin_t[r] = jnp.sin(angle)
+
+    for d in range(1, 4):
+        source, forward = x_forward(d)
+        arrived(x_slot(source), x_recv.at[source])
+        forward.start()
+    arrived(x_slot(sibling), x_recv.at[sibling])
+    for d in range(1, 4):
+        source = lax.rem(chip + 4 - d, 4) * 2 + (1 - core)
+        arrived(x_slot(source), x_recv.at[source])
+
+    def product(index):
+        part = xbuf[:, :, pl.ds(pl.multiple_of(index * depth, depth), depth)]
+        return jnp.dot(
+            part.reshape(2 * span, depth), wbuf[index], preferred_element_type=jnp.float32
+        )
+
+    total = product(plane)
+
+    def c_forward(d):
+        source = lax.rem(me + 8 - d, 8)
+        slot = c_slot(core, source)
+        return source, slot, remote(slot, slot, f_send.at[d], f_recv.at[source], sibling)
+
+    for d in [0] + list(range(1, 8)):
+        source, slot, forward = c_forward(d)
+        arrived(slot, c_recv.at[source])
+        forward.start()
+
+    for d in range(1, planes):
+        source = lax.rem(plane + d, planes)
+        arrived(wbuf.at[source], z_recv.at[source])
+        total = total + product(source)
+
+    half = HEAD // 2
+    for r in range(2):
+        first = total[r * span : (r + 1) * span, :half]
+        second = total[r * span : (r + 1) * span, half:]
+        cosine, sine = cos_t[r], sin_t[r]
+        stage[r, :, :half] = (first * cosine - second * sine).astype(jnp.bfloat16)
+        stage[r, :, half:] = (second * cosine + first * sine).astype(jnp.bfloat16)
+
+    def exchange(act):
+        @pl.when(core == 0)
+        def _():
+            for r in range(2):
+                act(
+                    stage.at[r],
+                    nbuf.at[0],
+                    n_send.at[r],
+                    n_recv.at[0],
+                    (2 * group + r) * 2 + lane,
+                )
+
+        @pl.when(core == 1)
+        def _():
+            for r in range(2):
+                for k in range(2):
+                    act(
+                        stage.at[r],
+                        nbuf.at[1 + lane],
+                        n_send.at[2 * r + k],
+                        n_recv.at[1 + lane],
+                        (2 * group + r) * 2 + k,
+                    )
+
+    def new_rows(act):
+        @pl.when(core == 1)
+        def _():
+            for which, out in ((0, nk), (1, nv)):
+
+                @pl.when(lane == which)
+                def _():
+                    for d in range(8):
+                        peer = lax.rem(me + d, 8)
+                        begin = pl.multiple_of(peer * slice_len, slice_len)
+                        act(
+                            stage.at[:, pl.ds(begin, slice_len), :],
+                            out.at[:, :, cols(group)],
+                            o_send.at[d],
+                            o_recv.at[2 * which + group],
+                            peer,
+                        )
+
+    exchange(push)
+    new_rows(push)
+
+    length = lens[lane]
+    arrived(nbuf.at[0], n_recv.at[0])
+    queries = nbuf[0]
+    contract = (((1,), (1,)), ((), ()))
+    scale = HEAD ** (-0.5)
+    for s in range(8):
+        arrived(c_slot(1 - core, s), f_recv.at[s])
+    top = jnp.full((span, 1), MASKED, jnp.float32)
+    for s in range(8):
+        scores = scale * lax.dot_general(
+            queries,
+            kvbuf[0, s * block : (s + 1) * block, :],
+            contract,
+            preferred_element_type=jnp.float32,
+        )
+        spot = s * block + lax.broadcasted_iota(jnp.int32, (span, block), 1)
+        scores = jnp.where(spot < length, scores, MASKED)
+        sbuf[s] = scores
+        top = jnp.maximum(top, jnp.max(scores, axis=-1, keepdims=True))
+    arrived(nbuf.at[1], n_recv.at[1])
+    scores = scale * lax.dot_general(
+        queries, nbuf[1], contract, preferred_element_type=jnp.float32
+    )
+    live = lax.broadcasted_iota(jnp.int32, (span, span), 1) <= lax.broadcasted_iota(
+        jnp.int32, (span, span), 0
+    )
+    scores = jnp.where(live, scores, MASKED)
+    top = jnp.maximum(top, jnp.max(scores, axis=-1, keepdims=True))
+    weights = jnp.exp(scores - top)
+    sums = jnp.sum(weights, axis=-1, keepdims=True)
+    arrived(nbuf.at[2], n_recv.at[2])
+    summed = jnp.dot(weights.astype(jnp.bfloat16), nbuf[2], preferred_element_type=jnp.float32)
+    for s in range(8):
+        weights = jnp.exp(sbuf[s] - top)
+        sums = sums + jnp.sum(weights, axis=-1, keepdims=True)
+        summed = summed + jnp.dot(
+            weights.astype(jnp.bfloat16),
+            kvbuf[1, s * block : (s + 1) * block, :],
+            preferred_element_type=jnp.float32,
+        )
+    ostage[...] = (summed / sums).astype(jnp.bfloat16)
+
+    def attended(act):
+        for d in list(range(1, 8)) + [0]:
+            peer = lax.rem(me + d, 8)
+            begin = pl.multiple_of(peer * slice_len, slice_len)
+            act(
+                ostage.at[pl.ds(begin, slice_len), :],
+                att.at[lane, :, cols(2 * group + core)],
+                a_send.at[d],
+                a_recv.at[me],
+                peer,
+            )
+
+    attended(push)
+
+    for d in range(1, 8):
+        peer = lax.rem(me + d, 8)
+        drain(w_slot(me), w_slot(me), w_send.at[d], w_recv.at[me], peer)
+        drain(c_slot(0, me), c_slot(0, me), c_send.at[d], c_recv.at[me], peer)
+    for d in range(1, planes):
+        z_copy(d).wait_send()
+    for d in range(4):
+        x_copy(d).wait_send()
+    for d in range(1, 4):
+        x_forward(d)[1].wait_send()
+    for d in range(8):
+        c_forward(d)[2].wait_send()
+    exchange(drain)
+    new_rows(drain)
+    attended(drain)
+    for which, out in ((0, nk), (1, nv)):
+        for g in range(2):
+            arrived(out.at[:, :, g * HEAD : (g + 1) * HEAD], o_recv.at[2 * which + g])
+    for s in range(8):
+        s_chip = s // 2
+        head = s_chip // 2 * 2 + s % 2
+        arrived(att.at[s_chip % 2, :, head * HEAD : (head + 1) * HEAD], a_recv.at[s])
+
+
+def fused_body(
+    planes, hidden_in, norm_gain, w_query, w_key, w_value, cache_keys, cache_values, cache_lengths
+):
+    requests, slice_len, width = hidden_in.shape
+    block = cache_keys.shape[1]
+    span = slice_len * 8
+    w_rows = w_query.shape[0]
+    frequency = (THETA ** (-(np.arange(HEAD // 2) * 2.0 / HEAD))).astype(np.float32)[None]
+    vmem = pl.BlockSpec(memory_space=pltpu.VMEM)
+    hbm = pl.BlockSpec(memory_space=pl.ANY)
+    smem = pl.BlockSpec(memory_space=pltpu.SMEM)
+    dma = pltpu.SemaphoreType.DMA
+    half = jnp.bfloat16
+    return tuple(
+        pl.pallas_call(
+            functools.partial(fused_kernel, planes),
+            out_shape=(
+                jax.ShapeDtypeStruct((requests, slice_len, HEADS * HEAD), half),
+                jax.ShapeDtypeStruct((requests, slice_len, KV_HEADS * HEAD), half),
+                jax.ShapeDtypeStruct((requests, slice_len, KV_HEADS * HEAD), half),
+            ),
+            in_specs=[hbm, vmem, vmem, hbm, hbm, hbm, hbm, hbm, smem],
+            out_specs=(hbm, hbm, hbm),
+            scratch_shapes=[
+                pltpu.VMEM((requests, slice_len, width), half),
+                pltpu.VMEM((requests, span, width), half),
+                pltpu.VMEM((planes, 8 * w_rows, HEAD), half),
+                pltpu.VMEM((2, 8 * block, HEAD), half),
+                pltpu.VMEM((requests, span, HEAD), half),
+                pltpu.VMEM((3, span, HEAD), half),
+                pltpu.VMEM((span, HEAD), half),
+                pltpu.VMEM((8, span, block), jnp.float32),
+                pltpu.VMEM((requests, span, HEAD // 2), jnp.float32),
+                pltpu.VMEM((requests, span, HEAD // 2), jnp.float32),
+                dma,
+                dma((8,)),
+                dma((8,)),
+                dma((planes,)),
+                dma((planes,)),
+                dma((7,)),
+                dma((8,)),
+                dma((8,)),
+                dma((8,)),
+                dma((8,)),
+                dma((8,)),
+                dma((4,)),
+                dma((3,)),
+                dma((8,)),
+                dma((4,)),
+                dma((8,)),
+                dma((8,)),
+            ],
+            compiler_params=pltpu.CompilerParams(
+                collective_id=0, has_side_effects=True, vmem_limit_bytes=40 * 1024 * 1024
+            ),
+        )(
+            hidden_in,
+            norm_gain[None],
+            jnp.asarray(frequency),
+            w_query,
+            w_key,
+            w_value,
+            cache_keys,
+            cache_values,
+            cache_lengths,
+        )
+    )
+
 
 def solution(mesh):
     in_specs = (
@@ -164,4 +584,7 @@
         P("req"),
     )
     out_specs = (P("req", "seq", None), P("req", "seq", None), P("req", "seq", None))
-    return jax.shard_map(body, mesh=mesh, in_specs=in_specs, out_specs=out_specs, check_vma=False)
+    program = body
+    if mesh.shape["seq"] == HEADS + 2 * KV_HEADS:
+        program = functools.partial(fused_body, mesh.shape["req"])
+    return jax.shard_map(program, mesh=mesh, in_specs=in_specs, out_specs=out_specs, check_vma=False)

time: 269 us -> 56.2 us (0.21)
  the two profiles are of different devices: /device:TPU:0 before, /device:TPU:9 now
where the time goes in v1:
time: 56.2 us; the launch traced here: 55.8 us
  Pallas kernels  46.3 us (82%)
  local copies, waits for them, and re-layouts  8.88 us (16%)
  between operations  0.67 us (1%)
    pallas_call x1, Pallas kernels, fused_body(): pl.pallas_call(functools.partial(fused_kernel, planes), out_shape=(jax.Sh...  46.3 us
    unnamed x21, local copies, waits for them, and re-layouts  8.88 us

profile of v1, /device:TPU:9, one launch (start us, length us, event | category | flops | bytes accessed | tf_op | source)
XLA Modules:
  0.0 55.8 jit_solution(1884451228325413869)
XLA Ops:
  0.6 0.0 copy-start.8
  0.6 0.0 copy-start.7
  0.7 0.6 %copy-done.8 = f32[1,128]{1,0:T(1,128)S(1)} copy-done((f32[1,128]{1,0:T(1,128)S(1)}, f32[1,128]{1,0:T(1,128)}, u32[]{:S(2)}) %copy-start.8) | copy-done | bytes 536
  1.3 0.0 copy-done.7
  1.3 0.0 copy-start
  1.3 1.0 %copy-done = bf16[2,256,512]{2,1,0:T(8,128)(2,1)S(1)} copy-done((bf16[2,256,512]{2,1,0:T(8,128)(2,1)S(1)}, bf16[2,256,512]{2,1,0:T(8,128)(2,1)}, u32[]{:S(2)}) %copy-start) | copy-done | bytes 524312
  2.4 0.0 copy-start.1
  2.4 1.0 %copy-done.1 = bf16[2,256,512]{2,1,0:T(8,128)(2,1)S(1)} copy-done((bf16[2,256,512]{2,1,0:T(8,128)(2,1)S(1)}, bf16[2,256,512]{2,1,0:T(8,128)(2,1)}, u32[]{:S(2)}) %copy-start.1) | copy-done | bytes 524312
  3.4 0.0 copy-start.2
  3.4 0.9 %copy-done.2 = bf16[2,32,2048]{2,1,0:T(8,128)(2,1)S(1)} copy-done((bf16[2,32,2048]{2,1,0:T(8,128)(2,1)S(1)}, bf16[2,32,2048]{2,1,0:T(8,128)(2,1)}, u32[]{:S(2)}) %copy-start.2) | copy-done | bytes 262168
  4.3 0.0 copy-start.3
  4.3 0.9 %copy-done.3 = bf16[64,1024]{1,0:T(8,128)(2,1)S(1)} copy-done((bf16[64,1024]{1,0:T(8,128)(2,1)S(1)}, bf16[64,1024]{1,0:T(8,128)(2,1)}, u32[]{:S(2)}) %copy-start.3) | copy-done | bytes 131096
  5.2 0.0 copy-start.4
  5.2 0.8 %copy-done.4 = bf16[64,512]{1,0:T(8,128)(2,1)S(1)} copy-done((bf16[64,512]{1,0:T(8,128)(2,1)S(1)}, bf16[64,512]{1,0:T(8,128)(2,1)}, u32[]{:S(2)}) %copy-start.4) | copy-done | bytes 65560
  6.1 0.0 copy-start.5
  6.1 0.8 %copy-done.5 = bf16[64,512]{1,0:T(8,128)(2,1)S(1)} copy-done((bf16[64,512]{1,0:T(8,128)(2,1)S(1)}, bf16[64,512]{1,0:T(8,128)(2,1)}, u32[]{:S(2)}) %copy-start.5) | copy-done | bytes 65560
  6.9 0.0 copy-start.6
  6.9 0.7 %copy-done.6 = f32[2048]{0:T(1024)S(1)} copy-done((f32[2048]{0:T(1024)S(1)}, f32[2048]{0:T(1024)}, u32[]{:S(2)}) %copy-start.6) | copy-done | bytes 8216
  7.6 46.3 %shard_map.112 = (bf16[2,32,1024]{2,1,0:T(8,128)(2,1)S(1)}, bf16[2,32,512]{2,1,0:T(8,128)(2,1)S(1)}, bf16[2,32,512]{2,1,0:T(8,128)(2,1)S(1)}) custom-call(bf16[2,32,2048]{2,1,0:T(8,128)(2,1)S(1)} %copy-done.2, f32[1,2048]{1,0:T(1,128)S(1)} %bitcast.1, f32[1,128]{1,0:T(1,128)S(1)} %copy-done.8, bf16[64,1024]{1,0:T(8,128)(2,1)S(1)} %copy-done.3, ...), custom_call_target="tpu_custom_call" | custom-call | tf_op jit(solution)/shard_map/pallas_call | solution.py:520
  53.9 0.7 %copy.15 = bf16[2,32,1024]{2,1,0:T(8,128)(2,1)} copy(bf16[2,32,1024]{2,1,0:T(8,128)(2,1)S(1)} %get-tuple-element.6) | data formatting | bytes 262144
  54.6 0.6 %copy.16 = bf16[2,32,512]{2,1,0:T(8,128)(2,1)} copy(bf16[2,32,512]{2,1,0:T(8,128)(2,1)S(1)} %get-tuple-element.7) | data formatting | bytes 131072
  55.2 0.6 %copy.17 = bf16[2,32,512]{2,1,0:T(8,128)(2,1)} copy(bf16[2,32,512]{2,1,0:T(8,128)(2,1)S(1)} %get-tuple-element.8) | data formatting | bytes 131072
Async XLA Ops:
  0.6 0.7 %copy-start.8 = (f32[1,128]{1,0:T(1,128)S(1)}, f32[1,128]{1,0:T(1,128)}, u32[]{:S(2)}) copy-start(f32[1,128]{1,0:T(1,128)} %constant.2.clone.freq_ref) | copy-start | bytes 1540
  0.6 0.7 %copy-start.7 = (s32[2]{0:T(128)S(1)}, s32[2]{0:T(128)}, u32[]{:S(2)}) copy-start(s32[2]{0:T(128)} %lens.1) | copy-start | bytes 28
  1.3 1.0 %copy-start = (bf16[2,256,512]{2,1,0:T(8,128)(2,1)S(1)}, bf16[2,256,512]{2,1,0:T(8,128)(2,1)}, u32[]{:S(2)}) copy-start(bf16[2,256,512]{2,1,0:T(8,128)(2,1)} %ck.1) | copy-start | bytes 1572868
  2.4 1.0 %copy-start.1 = (bf16[2,256,512]{2,1,0:T(8,128)(2,1)S(1)}, bf16[2,256,512]{2,1,0:T(8,128)(2,1)}, u32[]{:S(2)}) copy-start(bf16[2,256,512]{2,1,0:T(8,128)(2,1)} %cv.1) | copy-start | bytes 1572868
  3.4 0.9 %copy-start.2 = (bf16[2,32,2048]{2,1,0:T(8,128)(2,1)S(1)}, bf16[2,32,2048]{2,1,0:T(8,128)(2,1)}, u32[]{:S(2)}) copy-start(bf16[2,32,2048]{2,1,0:T(8,128)(2,1)} %x_hbm.1) | copy-start | bytes 786436
  4.3 0.9 %copy-start.3 = (bf16[64,1024]{1,0:T(8,128)(2,1)S(1)}, bf16[64,1024]{1,0:T(8,128)(2,1)}, u32[]{:S(2)}) copy-start(bf16[64,1024]{1,0:T(8,128)(2,1)} %wq.1) | copy-start | bytes 393220
  5.2 0.8 %copy-start.4 = (bf16[64,512]{1,0:T(8,128)(2,1)S(1)}, bf16[64,512]{1,0:T(8,128)(2,1)}, u32[]{:S(2)}) copy-start(bf16[64,512]{1,0:T(8,128)(2,1)} %wk.1) | copy-start | bytes 196612
  6.1 0.8 %copy-start.5 = (bf16[64,512]{1,0:T(8,128)(2,1)S(1)}, bf16[64,512]{1,0:T(8,128)(2,1)}, u32[]{:S(2)}) copy-start(bf16[64,512]{1,0:T(8,128)(2,1)} %wv.1) | copy-start | bytes 196612
  6.9 0.7 %copy-start.6 = (f32[2048]{0:T(1024)S(1)}, f32[2048]{0:T(1024)}, u32[]{:S(2)}) copy-start(f32[2048]{0:T(1024)} %param.10) | copy-start | bytes 24580

commit v2 on v1

--- a/solution.py
+++ b/solution.py
@@ -162,8 +162,8 @@
 def fused_kernel(
     planes,
     x_hbm,
-    gain_ref,
-    freq_ref,
+    gain_hbm,
+    freq_hbm,
     wq,
     wk,
     wv,
@@ -173,6 +173,8 @@
     att,
     nk,
     nv,
+    gain_ref,
+    freq_ref,
     xin,
     xbuf,
     wbuf,
@@ -242,8 +244,14 @@
     def arrived(dst, rsem):
         pltpu.make_async_copy(dst, dst, rsem).wait()
 
-    load_x = pltpu.make_async_copy(x_hbm, xin, xin_sem)
-    load_x.start()
+    loads = [
+        pltpu.make_async_copy(source, target, xin_sem.at[index])
+        for index, (source, target) in enumerate(
+            ((x_hbm, xin), (gain_hbm, gain_ref), (freq_hbm, freq_ref))
+        )
+    ]
+    for load in loads:
+        load.start()
     barrier = pltpu.get_barrier_semaphore()
     for d in range(1, 8):
         pl.semaphore_signal(
@@ -253,7 +261,8 @@
         pl.semaphore_signal(
             barrier, inc=1, device_id={"req": lax.rem(plane + d, planes)}, device_id_type=MESH_ID
         )
-    load_x.wait()
+    for load in loads:
+        load.wait()
     rows = xin[...].astype(jnp.float32)
     mean = jnp.mean(rows * rows, axis=-1, keepdims=True)
     normed = (rows * lax.rsqrt(mean + EPSILON) * gain_ref[...][None]).astype(jnp.bfloat16)
@@ -285,17 +294,30 @@
     def x_slot(source):
         return xbuf.at[:, pl.ds(pl.multiple_of(source * slice_len, slice_len), slice_len), :]
 
+    beside, across, far = chip + 1 - 2 * lane, lax.rem(chip + 2, 4), 3 - chip
+
     def x_copy(d):
-        peer = lax.rem(chip + d, 4) * 2 + core if d else sibling
+        peer = (sibling, beside * 2 + core, across * 2 + core)[d]
         return remote(x_slot(me), x_slot(me), x_send.at[d], x_recv.at[me], peer)
 
+    def x_half(source, part):
+        return xbuf.at[
+            part, pl.ds(pl.multiple_of(source * slice_len, slice_len), slice_len), :
+        ]
+
+    def x_relay(d):
+        source = (beside if d == 0 else across) * 2 + core
+        peer = (across if d == 0 else beside) * 2 + core
+        slot = x_half(source, d)
+        return remote(slot, slot, x_send.at[3 + d], (x_recv.at[source], x_recv.at[8])[d], peer)
+
     def x_forward(d):
-        source = lax.rem(chip + 4 - d, 4) * 2 + core
+        source = (far, beside, across)[d] * 2 + core
         return source, remote(
-            x_slot(source), x_slot(source), x_send.at[3 + d], x_recv.at[source], sibling
-        )
-
-    for d in (1, 2, 3, 0):
+            x_slot(source), x_slot(source), x_send.at[5 + d], x_recv.at[source], sibling
+        )
+
+    for d in (1, 2, 0):
         x_copy(d).start()
 
     def c_slot(which, source):
@@ -327,8 +349,40 @@
             device_id_type=MESH_ID,
         )
 
-    for d in range(1, planes):
-        z_copy(d).start()
+    relayed = 3 * (2 - plane) if planes == 4 else planes
+
+    def z_direct(act):
+        for d in (2, 1, 3) if planes == 4 else range(1, planes):
+            if planes == 4 and d != 2:
+
+                @pl.when(lax.abs(lax.rem(plane + d, planes) - plane) != 3)
+                def _():
+                    act(z_copy(d))
+
+            else:
+                act(z_copy(d))
+
+    def z_relay(act):
+        if planes == 4:
+
+            @pl.when((plane == 1) | (plane == 2))
+            def _():
+                act(
+                    pltpu.make_async_remote_copy(
+                        src_ref=wbuf.at[relayed],
+                        dst_ref=wbuf.at[relayed],
+                        send_sem=z_send.at[0],
+                        recv_sem=z_recv.at[relayed],
+                        device_id={"req": 3 - relayed},
+                        device_id_type=MESH_ID,
+                    )
+                )
+
+    def z_pass(copy):
+        arrived(wbuf.at[relayed], z_recv.at[relayed])
+        copy.start()
+
+    z_direct(lambda copy: copy.start())
 
     is_value = core * lane
     turn = (1 - is_value).astype(jnp.float32)
@@ -338,10 +392,16 @@
         cos_t[r] = jnp.cos(angle)
         sin_t[r] = jnp.sin(angle)
 
-    for d in range(1, 4):
+    for d in (1, 2):
         source, forward = x_forward(d)
         arrived(x_slot(source), x_recv.at[source])
+        x_relay(d - 1).start()
         forward.start()
+    z_relay(z_pass)
+    source, forward = x_forward(0)
+    arrived(x_half(source, 0), x_recv.at[source])
+    arrived(x_half(source, 1), x_recv.at[8])
+    forward.start()
     arrived(x_slot(sibling), x_recv.at[sibling])
     for d in range(1, 4):
         source = lax.rem(chip + 4 - d, 4) * 2 + (1 - core)
@@ -367,7 +427,11 @@
 
     for d in range(1, planes):
         source = lax.rem(plane + d, planes)
-        arrived(wbuf.at[source], z_recv.at[source])
+
+        @pl.when(source != relayed)
+        def _():
+            arrived(wbuf.at[source], z_recv.at[source])
+
         total = total + product(source)
 
     half = HEAD // 2
@@ -421,7 +485,6 @@
                         )
 
     exchange(push)
-    new_rows(push)
 
     length = lens[lane]
     arrived(nbuf.at[0], n_recv.at[0])
@@ -478,17 +541,19 @@
             )
 
     attended(push)
+    new_rows(push)
 
     for d in range(1, 8):
         peer = lax.rem(me + d, 8)
         drain(w_slot(me), w_slot(me), w_send.at[d], w_recv.at[me], peer)
         drain(c_slot(0, me), c_slot(0, me), c_send.at[d], c_recv.at[me], peer)
-    for d in range(1, planes):
-        z_copy(d).wait_send()
-    for d in range(4):
+    z_direct(lambda copy: copy.wait_send())
+    z_relay(lambda copy: copy.wait_send())
+    for d in range(3):
         x_copy(d).wait_send()
-    for d in range(1, 4):
         x_forward(d)[1].wait_send()
+    for d in range(2):
+        x_relay(d).wait_send()
     for d in range(8):
         c_forward(d)[2].wait_send()
     exchange(drain)
@@ -511,8 +576,8 @@
     span = slice_len * 8
     w_rows = w_query.shape[0]
     frequency = (THETA ** (-(np.arange(HEAD // 2) * 2.0 / HEAD))).astype(np.float32)[None]
-    vmem = pl.BlockSpec(memory_space=pltpu.VMEM)
-    hbm = pl.BlockSpec(memory_space=pl.ANY)
+    hbm = pl.BlockSpec(memory_space=pltpu.HBM)
+    anywhere = pl.BlockSpec(memory_space=pl.ANY)
     smem = pl.BlockSpec(memory_space=pltpu.SMEM)
     dma = pltpu.SemaphoreType.DMA
     half = jnp.bfloat16
@@ -524,9 +589,11 @@
                 jax.ShapeDtypeStruct((requests, slice_len, KV_HEADS * HEAD), half),
                 jax.ShapeDtypeStruct((requests, slice_len, KV_HEADS * HEAD), half),
             ),
-            in_specs=[hbm, vmem, vmem, hbm, hbm, hbm, hbm, hbm, smem],
-            out_specs=(hbm, hbm, hbm),
+            in_specs=[hbm, hbm, hbm, hbm, hbm, hbm, hbm, hbm, smem],
+            out_specs=(anywhere, anywhere, anywhere),
             scratch_shapes=[
+                pltpu.VMEM((1, width), jnp.float32),
+                pltpu.VMEM((1, HEAD // 2), jnp.float32),
                 pltpu.VMEM((requests, slice_len, width), half),
                 pltpu.VMEM((requests, span, width), half),
                 pltpu.VMEM((planes, 8 * w_rows, HEAD), half),
@@ -537,13 +604,13 @@
                 pltpu.VMEM((8, span, block), jnp.float32),
                 pltpu.VMEM((requests, span, HEAD // 2), jnp.float32),
                 pltpu.VMEM((requests, span, HEAD // 2), jnp.float32),
-                dma,
+                dma((3,)),
                 dma((8,)),
                 dma((8,)),
                 dma((planes,)),
                 dma((planes,)),
-                dma((7,)),
-                dma((8,)),
+                dma((8,)),
+                dma((9,)),
                 dma((8,)),
                 dma((8,)),
                 dma((8,)),
@@ -556,7 +623,7 @@
                 dma((8,)),
             ],
             compiler_params=pltpu.CompilerParams(
-                collective_id=0, has_side_effects=True, vmem_limit_bytes=40 * 1024 * 1024
+                collective_id=0, has_side_effects=True, vmem_limit_bytes=64 * 1024 * 1024
             ),
         )(
             hidden_in,

time: 56.2 us -> 48.9 us (0.87)
  the two profiles are of different devices: /device:TPU:9 before, /device:TPU:0 now
where the time goes in v2:
time: 48.9 us; the launch traced here: 48.7 us
  Pallas kernels  44.9 us (92%)
  local copies, waits for them, and re-layouts  3.09 us (6%)
  between operations  0.65 us (1%)
    pallas_call x1, Pallas kernels, fused_body(): pl.pallas_call(functools.partial(fused_kernel, planes), out_shape=(jax.Sh...  44.9 us
    unnamed x7, local copies, waits for them, and re-layouts  3.09 us

profile of v2, /device:TPU:0, one launch (start us, length us, event | category | flops | bytes accessed | tf_op | source)
XLA Modules:
  0.0 48.7 jit_solution(5164703603035108888)
XLA Ops:
  0.6 44.9 %shard_map.112 = (bf16[2,32,1024]{2,1,0:T(8,128)(2,1)}, bf16[2,32,512]{2,1,0:T(8,128)(2,1)}, bf16[2,32,512]{2,1,0:T(8,128)(2,1)}) custom-call(bf16[2,32,2048]{2,1,0:T(8,128)(2,1)} %x_hbm.1, f32[1,2048]{1,0:T(1,128)} %bitcast.1, f32[1,128]{1,0:T(1,128)} %constant.2.clone.freq_hbm, bf16[64,1024]{1,0:T(8,128)(2,1)} %wq.1, bf16[64,512]{1,0:T(8,128)(2,1)} %wk.1, ...), custom_call_target="tpu_custom_call" | custom-call | tf_op jit(solution)/shard_map/pallas_call | solution.py:585
  45.6 0.0 copy-start.1
  45.6 1.6 %copy.15 = bf16[2,32,1024]{2,1,0:T(8,128)(2,1)} copy(bf16[2,32,1024]{2,1,0:T(8,128)(2,1)} %get-tuple-element.6) | data formatting | bytes 262144
  47.2 0.0 copy-done.1
  47.2 0.0 copy-start
  47.2 0.6 %copy.16 = bf16[2,32,512]{2,1,0:T(8,128)(2,1)} copy(bf16[2,32,512]{2,1,0:T(8,128)(2,1)S(1)} %copy-done.1) | data formatting | bytes 131072
  47.8 0.2 copy-done
  48.0 0.6 %copy.17 = bf16[2,32,512]{2,1,0:T(8,128)(2,1)} copy(bf16[2,32,512]{2,1,0:T(8,128)(2,1)S(1)} %copy-done) | data formatting | bytes 131072
Async XLA Ops:
  45.6 1.6 %copy-start.1 = (bf16[2,32,512]{2,1,0:T(8,128)(2,1)S(1)}, bf16[2,32,512]{2,1,0:T(8,128)(2,1)}, u32[]{:S(2)}) copy-start(bf16[2,32,512]{2,1,0:T(8,128)(2,1)} %get-tuple-element.7) | copy-start | bytes 196612
  47.2 0.9 %copy-start = (bf16[2,32,512]{2,1,0:T(8,128)(2,1)S(1)}, bf16[2,32,512]{2,1,0:T(8,128)(2,1)}, u32[]{:S(2)}) copy-start(bf16[2,32,512]{2,1,0:T(8,128)(2,1)} %get-tuple-element.8) | copy-start | bytes 196612
